TPU v7x, 512 devices: a whole 4x4x16 slice. The times are simulated.
512 devices in a mesh: wide: 64 (over y, z), tp: 8 (over x, core).
Axes of the slice: x: 4, y: 4, z: 16, core: 2. Of those that a mesh axis runs over, the one named last changes fastest.
Arguments:
- hidden: bfloat16 [256, 2, 4096], P('wide'), may hold values from -6 to 6
- new_keys: bfloat16 [256, 2, 1024], P('wide', None, 'tp'), may hold values from -6 to 6
- key_cache: bfloat16 [256, 8, 512, 128], P('wide', 'tp'), may hold values from -700 to 700
- value_cache: bfloat16 [256, 8, 512, 128], P('wide', 'tp'), may hold values from -6 to 6
- cache_len: int32 [256], P('wide'), may hold values from 1 to 512
- adapter_id: int32 [256], P('wide'), may hold values from 0 to 255
- adapter_slot: int32 [256], replicated, may hold values from 0 to 255, each once
- adapter_rank: int32 [256], replicated, may hold values from 1 to 64
- q_weight: bfloat16 [4096, 2048], P(None, 'tp'), may hold values from -0.09375 to 0.09375
- v_weight: bfloat16 [4096, 1024], P(None, 'tp'), may hold values from -0.09375 to 0.09375
- q_down: bfloat16 [256, 4096, 64], P('wide', 'tp'), may hold values from -0.09375 to 0.09375
- v_down: bfloat16 [256, 4096, 64], P('wide', 'tp'), may hold values from -0.09375 to 0.09375
- q_up: bfloat16 [256, 64, 2048], P('wide', None, 'tp'), may hold values from -1 to 1
- v_up: bfloat16 [256, 64, 1024], P('wide', None, 'tp'), may hold values from -1 to 1
Outputs:
- attended: bfloat16 [256, 2, 2048], P('wide', None, 'tp')
- new_values: bfloat16 [256, 2, 1024], P('wide', None, 'tp')
Inputs may be any that keep to these rules, and one draw needn't show every extreme that they name: Adapter a is stored at slot adapter_slot[a], on the index adapter_slot[a] // 4 of wide, at position adapter_slot[a] % 4 there. Only the first adapter_rank[a] of the 64 columns of an adapter's first factors, and rows of its second factors, belong to it. The new tokens stand at positions cache_len and cache_len + 1.
All inputs are finite; a program needn't handle non-finite values.
Results may differ from a plain program's by a relative error of at most 0.014.
The roundings to bfloat16 on the way count: a program that leaves them out, or rounds other values in their place, can miss the bound.
Values may be sent and summed in bfloat16 or wider, within the bound.
A program may use at most 64 MiB of HBM per device.

v0:
```python
import math

import jax
import jax.numpy as jnp
from jax import lax
from jax.sharding import PartitionSpec as P


def sent_to_all(value, axis):
    copies = jnp.broadcast_to(value, (lax.axis_size(axis), *value.shape))
    return lax.all_to_all(copies, axis, split_axis=0, concat_axis=0, tiled=True)


def laid_out(tiles, dim):
    lengths = list(tiles.shape[1:])
    lengths[dim] *= tiles.shape[0]
    return jnp.moveaxis(tiles, 0, dim).reshape(lengths)


def gathered_copies(value, axis, dim):
    tiles = sent_to_all(value, axis)
    return laid_out(tiles, dim)


def taken_together(value, axis):
    return sent_to_all(value, axis).sum(axis=0)


def rotate(queries, position):
    head_dim = queries.shape[-1]
    half_width = head_dim // 2
    frequency = jnp.exp(
        -math.log(500000.0) * (2.0 * jnp.arange(half_width, dtype=jnp.float32) / head_dim)
    )
    angles = position.astype(jnp.float32)[:, :, None] * frequency
    cosine = jnp.cos(angles)[:, :, None, :]
    sine_part = jnp.sin(angles)[:, :, None, :]
    lower_half = queries[..., :half_width]
    second = queries[..., half_width:]
    return jnp.concatenate(
        [lower_half * cosine - second * sine_part, second * cosine + lower_half * sine_part], -1
    )


def local(
    hidden,
    new_keys,
    key_cache,
    value_cache,
    cache_len,
    adapter_id,
    adapter_slot,
    adapter_rank,
    q_weight,
    v_weight,
    q_down,
    v_down,
    q_up,
    v_up,
):
    tp_count = lax.axis_size("tp")
    tp_index = lax.axis_index("tp")
    owner_index = lax.axis_index("wide")
    rows_dev = hidden.shape[0]
    model_width = hidden.shape[2]
    slice_width = model_width // tp_count
    slots_dev = q_down.shape[0]
    rank_width = q_down.shape[2]
    q_width = q_up.shape[2]
    v_width = v_up.shape[2]
    adapters = adapter_slot.shape[0]
    all_ids = gathered_copies(adapter_id, "wide", 0)
    table_hits = all_ids[:, None] == jnp.arange(adapters, dtype=jnp.int32)[None, :]
    slot_index = jnp.sum(jnp.where(table_hits, adapter_slot[None, :], 0), 1)
    rank_value = jnp.sum(jnp.where(table_hits, adapter_rank[None, :], 0), 1)
    owned = slot_index // slots_dev == owner_index
    local_slot = slot_index % slots_dev
    chosen_slot = (
        (local_slot[:, None] == jnp.arange(slots_dev, dtype=jnp.int32)[None, :]) & owned[:, None]
    ).astype(jnp.float32)
    rank_mask = (jnp.arange(rank_width, dtype=jnp.int32)[None, :] < rank_value[:, None]).astype(
        jnp.float32
    )
    both_masks = jnp.concatenate([rank_mask, rank_mask], 1)
    features = lax.dynamic_slice_in_dim(hidden, tp_index * slice_width, slice_width, 2)
    down_table = jnp.concatenate([q_down, v_down], 2)
    down_table = jnp.transpose(down_table, (1, 0, 2)).reshape(
        slice_width, slots_dev * 2 * rank_width
    )
    shard_rows = gathered_copies(features, "wide", 0)
    row_count = shard_rows.shape[0]
    flat_rows = shard_rows.reshape(row_count * 2, slice_width)
    products = jnp.dot(flat_rows, down_table, preferred_element_type=jnp.float32)
    products = products.reshape(row_count, 2, slots_dev, 2 * rank_width)
    mixed = jnp.sum(products * chosen_slot[:, None, :, None], 2)
    partial_terms = mixed * both_masks[:, None, :]
    shrunk = taken_together(partial_terms, "tp").astype(jnp.bfloat16)
    total_rows = shrunk.shape[0]
    token_slots = jnp.repeat(chosen_slot, 2, 0).astype(jnp.bfloat16)

    def expand(reduced, up_table, width):
        spread = (reduced[:, None, :] * token_slots[:, :, None]).reshape(
            total_rows * 2, slots_dev * rank_width
        )
        return jnp.dot(
            spread,
            up_table.reshape(slots_dev * rank_width, width),
            preferred_element_type=jnp.float32,
        )

    flat_shrunk = shrunk.reshape(total_rows * 2, 2 * rank_width)
    delta_q = expand(flat_shrunk[:, :rank_width], q_up, q_width).astype(jnp.bfloat16)
    delta_v = expand(flat_shrunk[:, rank_width:], v_up, v_width).astype(jnp.bfloat16)
    adapter_delta = jnp.concatenate([delta_q, delta_v], 1).reshape(total_rows, 2, q_width + v_width)
    arrived = lax.all_to_all(adapter_delta, "wide", split_axis=0, concat_axis=0, tiled=True)
    row_delta = jnp.sum(arrived.reshape(-1, rows_dev, 2, q_width + v_width).astype(jnp.float32), 0)
    flat_hidden = hidden.reshape(rows_dev * 2, model_width)
    queries = (
        jnp.dot(flat_hidden, q_weight, preferred_element_type=jnp.float32).reshape(
            rows_dev, 2, q_width
        )
        + row_delta[:, :, :q_width]
    )
    new_values = (
        jnp.dot(flat_hidden, v_weight, preferred_element_type=jnp.float32).reshape(
            rows_dev, 2, v_width
        )
        + row_delta[:, :, q_width:]
    )
    new_values = new_values.astype(jnp.bfloat16)
    kv_local = key_cache.shape[1]
    cache_slots = key_cache.shape[2]
    head_dim = key_cache.shape[3]
    heads_local = q_width // head_dim
    group_size = heads_local // kv_local
    position = cache_len[:, None] + jnp.arange(2, dtype=jnp.int32)[None, :]
    queries = rotate(queries.reshape(rows_dev, 2, heads_local, head_dim), position).astype(
        jnp.bfloat16
    )
    queries = queries.reshape(rows_dev, 2, kv_local, group_size, head_dim)
    fresh_keys = new_keys.reshape(rows_dev, 2, kv_local, head_dim)
    fresh_values = new_values.reshape(rows_dev, 2, kv_local, head_dim)
    inv_root = 1.0 / math.sqrt(head_dim)
    old_scores = (
        jnp.einsum("rsghd,rgcd->rsghc", queries, key_cache, preferred_element_type=jnp.float32)
        * inv_root
    )
    live_slot = jnp.arange(cache_slots, dtype=jnp.int32)[None, :] < cache_len[:, None]
    old_scores = jnp.where(live_slot[:, None, None, None, :], old_scores, -jnp.inf)
    new_scores = (
        jnp.einsum("rsghd,rjgd->rsghj", queries, fresh_keys, preferred_element_type=jnp.float32)
        * inv_root
    )
    causal = jnp.arange(2)[None, :] <= jnp.arange(2)[:, None]
    new_scores = jnp.where(causal[None, :, None, None, :], new_scores, -jnp.inf)
    largest = jnp.maximum(jnp.max(old_scores, -1), jnp.max(new_scores, -1))
    old_weight = jnp.exp(old_scores - largest[..., None])
    new_weight = jnp.exp(new_scores - largest[..., None])
    denominator = jnp.sum(old_weight, -1) + jnp.sum(new_weight, -1)
    old_prob = (old_weight / denominator[..., None]).astype(jnp.bfloat16)
    new_prob = (new_weight / denominator[..., None]).astype(jnp.bfloat16)
    result = jnp.einsum(
        "rsghc,rgcd->rsghd", old_prob, value_cache, preferred_element_type=jnp.float32
    )
    result = result + jnp.einsum(
        "rsghj,rjgd->rsghd", new_prob, fresh_values, preferred_element_type=jnp.float32
    )
    attended = result.astype(jnp.bfloat16).reshape(rows_dev, 2, q_width)
    return (attended, new_values)


def solution(mesh):
    return jax.shard_map(
        local,
        mesh=mesh,
        in_specs=(
            P("wide", None, None),
            P("wide", None, "tp"),
            P("wide", "tp", None, None),
            P("wide", "tp", None, None),
            P("wide"),
            P("wide"),
            P(),
            P(),
            P(None, "tp"),
            P(None, "tp"),
            P("wide", "tp", None),
            P("wide", "tp", None),
            P("wide", None, "tp"),
            P("wide", None, "tp"),
        ),
        out_specs=(P("wide", None, "tp"), P("wide", None, "tp")),
        check_vma=False,
    )
```

profile of v0, /device:TPU:1, one launch (start us, length us, event | category | flops | bytes accessed | tf_op | source)
XLA Modules:
  0.0 146.6 jit_solution(18070019046780145887)
XLA Ops:
  0.6 1.4 broadcast_in_dim.48
  2.1 19.3 %all-to-all-start.1 = ((s32[64,1,4]{2,1,0:T(1,128)}), s32[64,1,4]{2,1,0:T(1,128)S(1)}, u32[]{:S(2)}, u32[]{:S(2)}) async-start(s32[64,1,4]{2,1,0:T(1,128)} %broadcast_in_dim.48), calls=%async_computation.1 | async-start | bytes 65536 | tf_op jit(solution)/shard_map/all_to_all | solution.py:11
  21.4 0.7 constant_dynamic-slice_fusion
  22.1 12.6 %all-to-all-done.1 = s32[64,1,4]{2,1,0:T(1,128)S(1)} async-done(((s32[64,1,4]{2,1,0:T(1,128)}), s32[64,1,4]{2,1,0:T(1,128)S(1)}, u32[]{:S(2)}, u32[]{:S(2)}) %all-to-all-start.1) | async-done | bytes 1056 | tf_op jit(solution)/shard_map/all_to_all | solution.py:11
  34.7 0.9 broadcast_in_dim.47
  35.6 4.6 %all-to-all-start = ((bf16[64,4,2,512]{3,1,2,0:T(4,128)(2,1)}), bf16[64,4,2,512]{3,1,2,0:T(4,128)(2,1)S(1)}, u32[]{:S(2)}, u32[]{:S(2)}) async-start(bf16[64,4,2,512]{3,1,2,0:T(4,128)(2,1)} %broadcast_in_dim.47), calls=%async_computation | async-start | bytes 1048576 | tf_op jit(solution)/shard_map/all_to_all | solution.py:11
  40.2 0.5 broadcast.191
  40.7 0.7 reduce.7
  41.6 0.9 select_reduce_fusion
  42.8 25.5 %all-to-all-done = bf16[64,4,2,512]{3,1,2,0:T(4,128)(2,1)S(1)} async-done(((bf16[64,4,2,512]{3,1,2,0:T(4,128)(2,1)}), bf16[64,4,2,512]{3,1,2,0:T(4,128)(2,1)S(1)}, u32[]{:S(2)}, u32[]{:S(2)}) %all-to-all-start) | async-done | bytes 524320 | tf_op jit(solution)/shard_map/all_to_all | solution.py:11
  68.6 1.5 %fusion.2 = f32[256,2,128]{2,0,1:T(8,128)S(1)} fusion(bf16[4,512,64]{1,2,0:T(8,128)(2,1)} %param.25, bf16[4,512,64]{1,2,0:T(8,128)(2,1)} %param.24, bf16[256,2,512,1]{2,0,1,3:T(8,128)(2,1)S(1)} %reshape.269, f32[256,4]{0,1:T(4,128)S(1)} %get-tuple-element.15), kind=kOutput, calls=%fused_computation.3 | convolution fusion | flops 269942784 | bytes 1314816 | tf_op jit(solution)/shard_map/dot_general | solution.py:93
  70.2 1.5 %broadcast_in_dim.56 = f32[8,256,2,128]{3,1,2,0:T(8,128)} broadcast(f32[256,2,128]{2,0,1:T(8,128)S(1)} %broadcast_multiply_fusion), dimensions={1,2,3} | broadcast | bytes 2359296 | tf_op jit(solution)/shard_map/broadcast_in_dim | solution.py:10
  71.7 9.0 %all-to-all-start.2 = ((f32[8,256,2,128]{3,1,2,0:T(8,128)}), f32[8,256,2,128]{3,1,2,0:T(8,128)}, u32[]{:S(2)}, u32[]{:S(2)}) async-start(f32[8,256,2,128]{3,1,2,0:T(8,128)} %broadcast_in_dim.56), calls=%async_computation.2 | async-start | bytes 4194304 | tf_op jit(solution)/shard_map/all_to_all | solution.py:11
  81.0 26.1 %all-to-all-done.2 = f32[8,256,2,128]{3,1,2,0:T(8,128)} async-done(((f32[8,256,2,128]{3,1,2,0:T(8,128)}), f32[8,256,2,128]{3,1,2,0:T(8,128)}, u32[]{:S(2)}, u32[]{:S(2)}) %all-to-all-start.2) | async-done | bytes 2097184 | tf_op jit(solution)/shard_map/all_to_all | solution.py:11
  107.1 1.7 %reduce_sum.66 = bf16[256,2,128]{2,0,1:T(8,128)(2,1)S(1)} reduce(f32[8,256,2,128]{3,1,2,0:T(8,128)} %all-to-all-done.2, f32[]{:T(128)} %constant.52.clone.1), dimensions={0}, to_apply=%region_3.4 | reduce | flops 458752 | bytes 2228228 | tf_op jit(solution)/shard_map/reduce_sum | solution.py:26
  109.3 0.3 fusion.3
  110.1 0.9 reshape.260
  111.0 6.2 %all-to-all-start.3 = ((bf16[256,2,384]{2,1,0:T(2,128)(2,1)}), bf16[256,2,384]{2,1,0:T(2,128)(2,1)S(1)}, u32[]{:S(2)}, u32[]{:S(2)}) async-start(bf16[256,2,384]{2,1,0:T(2,128)(2,1)} %reshape.260), calls=%async_computation.3 | async-start | bytes 786432 | tf_op jit(solution)/shard_map/all_to_all | solution.py:115
  117.5 23.9 %all-to-all-done.3 = bf16[256,2,384]{2,1,0:T(2,128)(2,1)S(1)} async-done(((bf16[256,2,384]{2,1,0:T(2,128)(2,1)}), bf16[256,2,384]{2,1,0:T(2,128)(2,1)S(1)}, u32[]{:S(2)}, u32[]{:S(2)}) %all-to-all-start.3) | async-done | bytes 393248 | tf_op jit(solution)/shard_map/all_to_all | solution.py:115
  141.4 0.3 convert_reduce_fusion
  141.8 0.4 fusion.8
  142.7 0.4 fusion.41
  144.1 1.5 %fusion.14 = bf16[4,2,128]{2,1,0:T(2,128)(2,1)S(1)} fusion(bf16[4,2,4096]{2,1,0:T(2,128)(2,1)S(1)} %copy-done.3, bf16[4096,128]{1,0:T(8,128)(2,1)} %param.23, f32[4,2,384]{2,1,0:T(2,128)S(1)} %convert_reduce_fusion), kind=kOutput, calls=%fused_computation.20 | convolution fusion | flops 8390656 | bytes 1120256 | tf_op jit(solution)/shard_map/dot_general | solution.py:125
  146.0 0.6 reshape.266
  (60 shorter events, 4.1 us)
Async XLA Ops:
  0.6 141.1 %copy-start = (bf16[4096,256]{1,0:T(8,128)(2,1)S(1)}, bf16[4096,256]{1,0:T(8,128)(2,1)}, u32[]{:S(2)}) copy-start(bf16[4096,256]{1,0:T(8,128)(2,1)} %param.22) | copy-start | bytes 6291460
  2.1 32.6 %all-to-all-start.1 = ((s32[64,1,4]{2,1,0:T(1,128)}), s32[64,1,4]{2,1,0:T(1,128)S(1)}, u32[]{:S(2)}, u32[]{:S(2)}) async-start(s32[64,1,4]{2,1,0:T(1,128)} %broadcast_in_dim.48), calls=%async_computation.1 | async-start | bytes 65536 | tf_op jit(solution)/shard_map/all_to_all | solution.py:11
  35.6 32.7 %all-to-all-start = ((bf16[64,4,2,512]{3,1,2,0:T(4,128)(2,1)}), bf16[64,4,2,512]{3,1,2,0:T(4,128)(2,1)S(1)}, u32[]{:S(2)}, u32[]{:S(2)}) async-start(bf16[64,4,2,512]{3,1,2,0:T(4,128)(2,1)} %broadcast_in_dim.47), calls=%async_computation | async-start | bytes 1048576 | tf_op jit(solution)/shard_map/all_to_all | solution.py:11
  71.7 35.4 %all-to-all-start.2 = ((f32[8,256,2,128]{3,1,2,0:T(8,128)}), f32[8,256,2,128]{3,1,2,0:T(8,128)}, u32[]{:S(2)}, u32[]{:S(2)}) async-start(f32[8,256,2,128]{3,1,2,0:T(8,128)} %broadcast_in_dim.56), calls=%async_computation.2 | async-start | bytes 4194304 | tf_op jit(solution)/shard_map/all_to_all | solution.py:11
  80.6 28.6 %copy-start.5 = (bf16[4,64,256]{2,1,0:T(8,128)(2,1)S(1)}, bf16[4,64,256]{2,1,0:T(8,128)(2,1)}, u32[]{:S(2)}) copy-start(bf16[4,64,256]{2,1,0:T(8,128)(2,1)} %param.26) | copy-start | bytes 393220
  80.8 28.8 %copy-start.6 = (bf16[4,64,128]{2,1,0:T(8,128)(2,1)S(1)}, bf16[4,64,128]{2,1,0:T(8,128)(2,1)}, u32[]{:S(2)}) copy-start(bf16[4,64,128]{2,1,0:T(8,128)(2,1)} %param.27) | copy-start | bytes 196612
  109.1 8.0 %copy-start.2 = (s32[4]{0:T(128)S(1)}, s32[4]{0:T(128)}, u32[]{:S(2)}) copy-start(s32[4]{0:T(128)} %param.18) | copy-start | bytes 52
  109.3 32.5 %copy-start.3 = (bf16[4,2,4096]{2,1,0:T(2,128)(2,1)S(1)}, bf16[4,2,4096]{2,1,0:T(2,128)(2,1)}, u32[]{:S(2)}) copy-start(bf16[4,2,4096]{2,1,0:T(2,128)(2,1)} %param.14) | copy-start | bytes 196612
  110.1 32.3 %copy-start.7 = (bf16[4,2,128]{2,1,0:T(2,128)(2,1)S(1)}, bf16[4,2,128]{2,1,0:T(2,128)(2,1)}, u32[]{:S(2)}) copy-start(bf16[4,2,128]{2,1,0:T(2,128)(2,1)} %param.15) | copy-start | bytes 6148
  110.1 32.6 %copy-start.1 = (bf16[4,1,512,128]{3,2,1,0:T(8,128)(2,1)S(1)}, bf16[4,1,512,128]{3,2,1,0:T(8,128)(2,1)}, u32[]{:S(2)}) copy-start(bf16[4,1,512,128]{3,2,1,0:T(8,128)(2,1)} %param.16) | copy-start | bytes 1572868
  111.0 30.5 %all-to-all-start.3 = ((bf16[256,2,384]{2,1,0:T(2,128)(2,1)}), bf16[256,2,384]{2,1,0:T(2,128)(2,1)S(1)}, u32[]{:S(2)}, u32[]{:S(2)}) async-start(bf16[256,2,384]{2,1,0:T(2,128)(2,1)} %reshape.260), calls=%async_computation.3 | async-start | bytes 786432 | tf_op jit(solution)/shard_map/all_to_all | solution.py:115
  141.8 3.8 %copy-start.4 = (bf16[4,1,512,128]{3,2,1,0:T(8,128)(2,1)S(1)}, bf16[4,1,512,128]{3,2,1,0:T(8,128)(2,1)}, u32[]{:S(2)}) copy-start(bf16[4,1,512,128]{3,2,1,0:T(8,128)(2,1)} %param.17) | copy-start | bytes 1572868
  145.6 1.0 copy-start.8
where the time goes:
time: 149 us; the launch traced here: 147 us
  waiting for transfers between devices  88.1 us (59%)
  starting transfers between devices  39.1 us (26%)
  local copies, waits for them, and re-layouts  8.66 us (6%)
  matrix products  4.99 us (3%)
  other arithmetic  4.82 us (3%)
    all_to_all x3, waiting for transfers between devices, sent_to_all(): return lax.all_to_all(copies, axis, split_axis=0, concat_axis=0, tiled=True)  64.2 us
    all_to_all x3, starting transfers between devices, sent_to_all(): return lax.all_to_all(copies, axis, split_axis=0, concat_axis=0, tiled=True)  32.9 us
    all_to_all x1, waiting for transfers between devices, local(): lax.all_to_all(adapter_delta, 'wide', split_axis=0, concat_axis=0, tiled=...  23.9 us
    all_to_all x1, starting transfers between devices, local(): lax.all_to_all(adapter_delta, 'wide', split_axis=0, concat_axis=0, tiled=...  6.19 us
    broadcast_in_dim x3, local copies, waits for them, and re-layouts, sent_to_all(): copies = jnp.broadcast_to(value, (lax.axis_size(axis), *value.shape))  3.85 us
  transfers between devices with their start and end apart: 4, of which 4 were waited for; matrix products, arithmetic and copies ran while one was open for 3% of the time, Pallas kernels for 0%

commit v1 on v0

v1 whole, which is shorter than its diff:
```python
import functools
import math

import jax
import jax.numpy as jnp
from jax import lax
from jax.experimental import pallas as pl
from jax.experimental.pallas import tpu as pltpu
from jax.sharding import PartitionSpec as P

MESH = pl.DeviceIdType.MESH
LANES = 128


def factors(wide):
    return (4, 4, wide // 16) if wide >= 32 else (2, 2, wide // 4)


def order_of(n):
    near = [d for d in (1, n - 1) if d < n]
    return list(dict.fromkeys(near + list(range(1, n))))


def kernel(
    dims,
    hidden,
    new_keys,
    key_cache,
    value_cache,
    cache_len,
    adapter_id,
    adapter_slot,
    adapter_rank,
    q_weight,
    v_weight,
    q_down,
    v_down,
    q_up,
    v_up,
    attended,
    new_values,
    hid,
    h32,
    h16,
    kv,
    vv,
    nk,
    len_s,
    id_s,
    slot_s,
    rank_s,
    wq,
    wv,
    down,
    upq,
    upv,
    feats,
    meta,
    locs,
    mixed,
    arrive_p,
    red,
    delta,
    r1,
    s1,
    r2,
    s2,
    r3,
    base,
    cos_t,
    sin_t,
    kn,
    vn,
    local_sem,
    p1_send,
    p1_recv,
    m1_send,
    m1_recv,
    p2_send,
    p2_recv,
    m2_send,
    m2_recv,
    p3_send,
    p3_recv,
    m3_send,
    m3_recv,
    rs_send,
    rs_recv,
    ag_send,
    ag_recv,
    d1_send,
    d1_recv,
    d2_send,
    d2_recv,
    d3_send,
    d3_recv,
):
    ny, nn, nf, nt = dims
    nh = nf // 2
    rows, _, width = hidden.shape
    toks = rows * 2
    part = width // nt
    slots = q_up.shape[0]
    rank_w = q_up.shape[1]
    q_w = q_up.shape[2]
    v_w = v_up.shape[2]
    cache = key_cache.shape[2]
    bf, f32 = jnp.bfloat16, jnp.float32

    wide = lax.axis_index("wide")
    tp = lax.axis_index("tp")
    y = lax.div(wide, nf * nn)
    z = lax.rem(wide, nf * nn)
    zf = lax.div(z, nn)
    zn = lax.rem(z, nn)

    def turn(i, d, n):
        return lax.rem(i + d, n)

    def y_peer(d):
        return (turn(y, d, ny) * (nf * nn) + z, tp)

    def n_peer(d):
        return (y * (nf * nn) + zf * nn + turn(zn, d, nn), tp)

    def f_peer(d):
        return (y * (nf * nn) + turn(zf, d, nf) * nn + zn, tp)

    def t_peer(d):
        return (wide, turn(tp, d, nt))

    a_of = (y, zn)
    b_of = (zn, y)
    a_peer = (y_peer, n_peer)
    b_peer = (n_peer, y_peer)
    n_ab = ny

    loads = {}

    def load(name, src, dst, i):
        c = pltpu.make_async_copy(src, dst, local_sem.at[i])
        c.start()
        loads[name] = c

    load("hid", hidden, hid, 0)
    load("id", adapter_id, id_s, 1)
    load("slot", adapter_slot, slot_s, 2)
    load("rank", adapter_rank, rank_s, 3)
    load("len", cache_len, len_s, 4)
    load("nk", new_keys, nk, 5)

    barrier = pltpu.get_barrier_semaphore()
    peers = (
        [f_peer(d) for d in range(1, nf)]
        + [n_peer(d) for d in range(1, nn)]
        + [y_peer(d) for d in range(1, ny)]
        + [t_peer(d) for d in range(1, nt)]
    )
    for p in peers:
        pl.semaphore_signal(barrier, inc=1, device_id=p, device_id_type=MESH)

    for k in range(slots):
        row = k * 2 * rank_w
        load(f"qd{k}", q_down.at[k], down.at[pl.ds(row, rank_w)], 8 + 4 * k)
        load(f"vd{k}", v_down.at[k], down.at[pl.ds(row + rank_w, rank_w)], 9 + 4 * k)
    load("wq", q_weight, wq, 6)
    load("wv", v_weight, wv, 7)
    upq[...] = jnp.zeros_like(upq)
    upv[...] = jnp.zeros_like(upv)
    for k in range(slots):
        row = k * 2 * rank_w
        load(f"qu{k}", q_up.at[k], upq.at[pl.ds(row, rank_w)], 10 + 4 * k)
        load(f"vu{k}", v_up.at[k], upv.at[pl.ds(row + rank_w, rank_w)], 11 + 4 * k)
    n0 = 8 + 4 * slots
    load("kc", key_cache, kv, n0)
    load("vc", value_cache, vv, n0 + 1)

    own_set = lax.div(zf, nh)
    own_h = lax.rem(zf, nh)
    own_a = jnp.where(own_set == 0, y, zn)
    own_b = jnp.where(own_set == 0, zn, y)
    loads["hid"].wait()
    for r in range(rows):
        col = pl.multiple_of(tp * part, part)
        h32[2 * r : 2 * r + 2, :part] = hid[r, :, pl.ds(col, part)].astype(f32)
    feats[own_set, own_a, own_b, own_h] = h32[:, :part].astype(bf)
    for name in ("id", "slot", "rank", "len"):
        loads[name].wait()
    lane1 = lax.broadcasted_iota(jnp.int32, (1, LANES), 1)
    code = jnp.zeros((1, LANES), jnp.int32)
    for r in range(rows):
        ident = id_s[r]
        code = jnp.where(lane1 == r, slot_s[ident] * 256 + rank_s[ident], code)
    meta[own_set, own_a, own_b, own_h] = code

    sends = []

    def send(src, dst, ssem, rsem, peer):
        c = pltpu.make_async_remote_copy(
            src_ref=src,
            dst_ref=dst,
            send_sem=ssem,
            recv_sem=rsem,
            device_id=peer,
            device_id_type=MESH,
        )
        c.start()
        sends.append(c)

    def arrived(ref, sem):
        pltpu.make_async_copy(ref, ref, sem).wait()

    pl.semaphore_wait(barrier, len(peers))

    own = (own_set, own_a, own_b, own_h)
    for d in order_of(nf):
        send(meta.at[own], meta.at[own], m1_send.at[d], m1_recv.at[d], f_peer(d))
        send(feats.at[own], feats.at[own], p1_send.at[d], p1_recv.at[d], f_peer(d))

    for r in range(rows):
        h32[2 * r : 2 * r + 2, :] = hid[r].astype(f32)
    h16[...] = h32[...].astype(bf)
    tok = lax.broadcasted_iota(jnp.int32, (toks, LANES), 0)
    lane = lax.broadcasted_iota(jnp.int32, (toks, LANES), 1)
    position = lax.rem(tok, 2)
    for r in range(rows):
        position = position + jnp.where(lax.div(tok, 2) == r, len_s[r], 0)
    half = lax.rem(lane, 64)
    frequency = jnp.exp(-math.log(500000.0) * (2.0 * half.astype(f32) / 128))
    angle = position.astype(f32) * frequency
    cos_t[...] = jnp.cos(angle)
    sine = jnp.sin(angle)
    sin_t[...] = jnp.where(lane < 64, -sine, sine)
    kn[...] = jnp.zeros_like(kn)
    vn[...] = jnp.zeros_like(vn)
    loads["nk"].wait()
    for r in range(rows):
        kn[2 * r : 2 * r + 2, :] = nk[r].astype(f32)

    for d in order_of(nf):
        zp = turn(zf, nf - d, nf)
        ps, ph = lax.div(zp, nh), lax.rem(zp, nh)
        pa = jnp.where(ps == 0, y, zn)
        pb = jnp.where(ps == 0, zn, y)
        arrived(meta.at[ps, pa, pb, ph], m1_recv.at[d])
        arrived(feats.at[ps, pa, pb, ph], p1_recv.at[d])

    for d in order_of(n_ab):
        for s in range(2):
            mine = (s, a_of[s], b_of[s])
            send(meta.at[mine], meta.at[mine], m2_send.at[s, d], m2_recv.at[s, d], b_peer[s](d))
            send(feats.at[mine], feats.at[mine], p2_send.at[s, d], p2_recv.at[s, d], b_peer[s](d))

    for name in ("wq", "wv"):
        loads[name].wait()
    base[:, :q_w] = jnp.dot(h16[...], wq[...], preferred_element_type=f32)

    for d in order_of(n_ab):
        for s in range(2):
            got = (s, a_of[s], turn(b_of[s], n_ab - d, n_ab))
            arrived(meta.at[got], m2_recv.at[s, d])
            arrived(feats.at[got], p2_recv.at[s, d])

    for d in order_of(n_ab):
        for s in range(2):
            mine = (s, a_of[s])
            send(meta.at[mine], meta.at[mine], m3_send.at[s, d], m3_recv.at[s, d], a_peer[s](d))
            send(feats.at[mine], feats.at[mine], p3_send.at[s, d], p3_recv.at[s, d], a_peer[s](d))

    half_toks = n_ab * nh * toks
    chunk = 2 * half_toks
    piece = chunk // nt

    def products(d):
        if d:
            for s in range(2):
                got = (s, turn(a_of[s], d, n_ab))
                arrived(meta.at[got], m3_recv.at[s, n_ab - d])
                arrived(feats.at[got], p3_recv.at[s, n_ab - d])
        else:
            for k in range(slots):
                loads[f"qd{k}"].wait()
                loads[f"vd{k}"].wait()
        for s in range(2):
            a = turn(a_of[s], d, n_ab)
            x = feats[s, a].reshape(half_toks, part)
            prod = lax.dot_general(
                x, down[...], (((1,), (1,)), ((), ())), preferred_element_type=f32
            )
            codes = meta[s, a].reshape(n_ab * nh, 1, LANES).astype(f32)
            codes = jnp.broadcast_to(codes, (n_ab * nh, toks, LANES))
            lane3 = lax.broadcasted_iota(jnp.int32, codes.shape, 2)
            tok3 = lax.broadcasted_iota(jnp.int32, codes.shape, 1)
            codes = jnp.where(lane3 == lax.div(tok3, 2), codes, 0.0)
            codes = jnp.sum(codes, -1, keepdims=True).reshape(half_toks, 1)
            codes = jnp.broadcast_to(codes, (half_toks, LANES)).astype(jnp.int32)
            rank = lax.rem(codes, 256)
            slot = lax.div(codes, 256)
            place = slot - wide * slots
            locs[d, s] = place
            total = jnp.zeros((half_toks, LANES), f32)
            for k in range(slots):
                total = jnp.where(place == k, prod[:, k * LANES : (k + 1) * LANES], total)
            col = lax.rem(lax.broadcasted_iota(jnp.int32, total.shape, 1), rank_w)
            total = jnp.where(col < rank, total, 0.0)
            n = nt // 2
            mixed[d, s * n : (s + 1) * n] = total.reshape(n, piece, LANES)
        for e in range(1, nt):
            send(
                mixed.at[d, turn(tp, e, nt)],
                arrive_p.at[d, e],
                rs_send.at[d, e],
                rs_recv.at[d, e],
                t_peer(e),
            )

    def reduce(d):
        total = mixed[d, tp]
        for e in range(1, nt):
            arrived(arrive_p.at[d, e], rs_recv.at[d, e])
            total = total + arrive_p[d, e]
        red[d, tp] = total.astype(bf)
        for e in range(1, nt):
            send(red.at[d, tp], red.at[d, tp], ag_send.at[d, e], ag_recv.at[d, e], t_peer(e))

    def expand(d):
        if d == 0:
            for k in range(slots):
                loads[f"qu{k}"].wait()
                loads[f"vu{k}"].wait()
        for e in range(1, nt):
            arrived(red.at[d, turn(tp, nt - e, nt)], ag_recv.at[d, e])
        n = nt // 2
        for s in range(2):
            shrunk = red[d, s * n : (s + 1) * n].reshape(half_toks, LANES).astype(f32)
            place = locs[d, s]
            spread = jnp.concatenate(
                [jnp.where(place == k, shrunk, 0.0).astype(bf) for k in range(slots)], 1
            )
            dq = jnp.dot(spread, upq[...], preferred_element_type=f32).astype(bf)
            dv = jnp.dot(spread, upv[...], preferred_element_type=f32).astype(bf)
            delta[d, s, :, :, :, :q_w] = dq.reshape(n_ab, nh, toks, q_w)
            delta[d, s, :, :, :, q_w:] = dv.reshape(n_ab, nh, toks, v_w)
            if d:
                send(delta.at[d, s], r1.at[s, d], d1_send.at[s, d], d1_recv.at[s, d], a_peer[s](d))

    order = [0] + order_of(n_ab)
    products(order[0])
    base[:, q_w:] = jnp.dot(h16[...], wv[...], preferred_element_type=f32)
    reduce(order[0])
    for i in range(1, len(order)):
        products(order[i])
        expand(order[i - 1])
        reduce(order[i])
    expand(order[-1])

    for s in range(2):
        total = delta[0, s].astype(f32)
        for d in order_of(n_ab):
            arrived(r1.at[s, d], d1_recv.at[s, d])
            total = total + r1[s, d].astype(f32)
        s1[s] = total.astype(bf)
        for d in order_of(n_ab):
            send(
                s1.at[s, turn(b_of[s], d, n_ab)],
                r2.at[s, d],
                d2_send.at[s, d],
                d2_recv.at[s, d],
                b_peer[s](d),
            )
    for s in range(2):
        total = s1[s, b_of[s]].astype(f32)
        for d in order_of(n_ab):
            arrived(r2.at[s, d], d2_recv.at[s, d])
            total = total + r2[s, d].astype(f32)
        s2[s * nh : (s + 1) * nh] = total.astype(bf)
    for d in order_of(nf):
        send(s2.at[turn(zf, d, nf)], r3.at[d], d3_send.at[d], d3_recv.at[d], f_peer(d))
    loads["kc"].wait()
    loads["vc"].wait()
    total = s2[zf].astype(f32)
    for d in order_of(nf):
        arrived(r3.at[d], d3_recv.at[d])
        total = total + r3[d].astype(f32)

    full = base[...] + total
    fresh = full[:, q_w:].astype(bf).astype(f32)
    vn[:toks, :] = fresh
    for r in range(rows):
        new_values[r] = fresh[2 * r : 2 * r + 2].astype(bf)
    heads = q_w // LANES
    turned = []
    for h in range(heads):
        x = full[:, h * LANES : (h + 1) * LANES]
        turned.append(x * cos_t[...] + pltpu.roll(x, 64, 1) * sin_t[...])
    queries = jnp.concatenate(turned, 0).astype(bf)
    many = heads * toks
    inv_root = 1.0 / math.sqrt(LANES)
    row_id = lax.broadcasted_iota(jnp.int32, (many, cache), 0)
    row_of = lax.div(lax.rem(row_id, toks), 2)
    spot = lax.broadcasted_iota(jnp.int32, (many, cache), 1)
    contract = (((1,), (1,)), ((), ()))
    scores = jnp.zeros((many, cache), f32)
    length = jnp.zeros((many, cache), jnp.int32)
    for r in range(rows):
        one = lax.dot_general(queries, kv[r, 0], contract, preferred_element_type=f32)
        scores = jnp.where(row_of == r, one, scores)
        length = jnp.where(row_of == r, len_s[r], length)
    scores = jnp.where(spot < length, scores * inv_root, -jnp.inf)
    fresh_scores = (
        lax.dot_general(queries, kn[...].astype(bf), contract, preferred_element_type=f32)
        * inv_root
    )
    row_n = lax.rem(lax.broadcasted_iota(jnp.int32, fresh_scores.shape, 0), toks)
    col_n = lax.broadcasted_iota(jnp.int32, fresh_scores.shape, 1)
    seen = (lax.div(row_n, 2) == lax.div(col_n, 2)) & (lax.rem(col_n, 2) <= lax.rem(row_n, 2))
    fresh_scores = jnp.where(seen, fresh_scores, -jnp.inf)
    largest = jnp.maximum(
        jnp.max(scores, -1, keepdims=True), jnp.max(fresh_scores, -1, keepdims=True)
    )
    old_weight = jnp.exp(scores - largest)
    new_weight = jnp.exp(fresh_scores - largest)
    denominator = jnp.sum(old_weight, -1, keepdims=True) + jnp.sum(new_weight, -1, keepdims=True)
    old_prob = old_weight / denominator
    new_prob = (new_weight / denominator).astype(bf)
    result = jnp.dot(new_prob, vn[...].astype(bf), preferred_element_type=f32)
    for r in range(rows):
        weights = jnp.where(row_of == r, old_prob, 0.0).astype(bf)
        result = result + jnp.dot(weights, vv[r, 0], preferred_element_type=f32)
    for r in range(rows):
        for h in range(heads):
            at = h * toks + 2 * r
            attended[r, :, h * LANES : (h + 1) * LANES] = result[at : at + 2].astype(bf)
    for c in sends:
        c.wait_send()


def local(dims, *args):
    (hidden, new_keys, key_cache, value_cache, cache_len, adapter_id, adapter_slot, adapter_rank,
     q_weight, v_weight, q_down, v_down, q_up, v_up) = args
    ny, nn, nf, nt = dims
    nh = nf // 2
    rows, _, width = hidden.shape
    toks = rows * 2
    part = width // nt
    slots, rank_w, q_w = q_up.shape
    v_w = v_up.shape[2]
    all_w = q_w + v_w
    piece = 2 * ny * nh * toks // nt
    half_toks = ny * nh * toks
    bf, f32, i32 = jnp.bfloat16, jnp.float32, jnp.int32
    V = pltpu.VMEM
    dma = pltpu.SemaphoreType.DMA
    q_down = jnp.swapaxes(q_down, 1, 2)
    v_down = jnp.swapaxes(v_down, 1, 2)
    scratch = [
        V((rows, 2, width), bf),
        V((toks, width), f32),
        V((toks, width), bf),
        V(key_cache.shape, bf),
        V(value_cache.shape, bf),
        V(new_keys.shape, bf),
        pltpu.SMEM(cache_len.shape, i32),
        pltpu.SMEM(adapter_id.shape, i32),
        pltpu.SMEM(adapter_slot.shape, i32),
        pltpu.SMEM(adapter_rank.shape, i32),
        V(q_weight.shape, bf),
        V(v_weight.shape, bf),
        V((slots * 2 * rank_w, part), bf),
        V((slots * 2 * rank_w, q_w), bf),
        V((slots * 2 * rank_w, v_w), bf),
        V((2, ny, ny, nh, toks, part), bf),
        V((2, ny, ny, nh, 1, LANES), i32),
        V((ny, 2, half_toks, LANES), i32),
        V((ny, nt, piece, LANES), f32),
        V((ny, nt, piece, LANES), f32),
        V((ny, nt, piece, LANES), bf),
        V((ny, 2, ny, nh, toks, all_w), bf),
        V((2, ny, ny, nh, toks, all_w), bf),
        V((2, ny, nh, toks, all_w), bf),
        V((2, ny, nh, toks, all_w), bf),
        V((nf, toks, all_w), bf),
        V((nf, toks, all_w), bf),
        V((toks, all_w), f32),
        V((toks, LANES), f32),
        V((toks, LANES), f32),
        V((LANES, LANES), f32),
        V((LANES, LANES), f32),
        dma((8 + 4 * slots + 2,)),
    ]
    for shape in ((nf,), (nf,), (2, ny), (2, ny), (2, ny), (2, ny), (ny, nt), (ny, nt),
                  (2, ny), (2, ny), (nf,)):
        scratch += [dma(shape), dma(shape)]
    any_space = pl.BlockSpec(memory_space=pl.ANY)
    vmem = pl.BlockSpec(memory_space=pltpu.VMEM)
    return tuple(
        pl.pallas_call(
            functools.partial(kernel, dims),
            out_shape=(
                jax.ShapeDtypeStruct((rows, 2, q_w), bf),
                jax.ShapeDtypeStruct((rows, 2, v_w), bf),
            ),
            in_specs=[any_space] * 14,
            out_specs=(vmem, vmem),
            scratch_shapes=scratch,
            compiler_params=pltpu.CompilerParams(
                collective_id=0, has_side_effects=True, vmem_limit_bytes=56 * 1024 * 1024
            ),
        )(hidden, new_keys, key_cache, value_cache, cache_len, adapter_id, adapter_slot,
          adapter_rank, q_weight, v_weight, q_down, v_down, q_up, v_up)
    )


def solution(mesh):
    dims = factors(mesh.shape["wide"]) + (mesh.shape["tp"],)
    return jax.shard_map(
        functools.partial(local, dims),
        mesh=mesh,
        in_specs=(
            P("wide", None, None),
            P("wide", None, "tp"),
            P("wide", "tp", None, None),
            P("wide", "tp", None, None),
            P("wide"),
            P("wide"),
            P(),
            P(),
            P(None, "tp"),
            P(None, "tp"),
            P("wide", "tp", None),
            P("wide", "tp", None),
            P("wide", None, "tp"),
            P("wide", None, "tp"),
        ),
        out_specs=(P("wide", None, "tp"), P("wide", None, "tp")),
        check_vma=False,
    )
```

time: 149 us -> 69.8 us (0.47)
  waiting for transfers between devices: 88.1 us -> 0 us
  Pallas kernels: 0 us -> 65.3 us
  starting transfers between devices: 39.1 us -> 0 us
  local copies, waits for them, and re-layouts: 8.66 us -> 2.5 us
  matrix products: 4.99 us -> 0 us
  other arithmetic: 4.82 us -> 0 us
    all_to_all x4 -> x0, waiting for transfers between devices: 88.1 us -> none  [the longest x3 64.2 us: sent_to_all(): return lax.all_to_all(copies, axis, split_axis=0, concat_axis=0, tiled=True)]
    pallas_call x0 -> x1, Pallas kernels: none -> 65.3 us  [local(): pl.pallas_call(functools.partial(kernel, dims), out_shape=(jax.ShapeDtype...]
    all_to_all x4 -> x0, starting transfers between devices: 39.1 us -> none  [the longest x3 32.9 us: sent_to_all(): return lax.all_to_all(copies, axis, split_axis=0, concat_axis=0, tiled=True)]
    dot_general x9 -> x0, matrix products: 4.99 us -> none  [the longest x1 1.53 us: local(): jnp.dot(flat_rows, down_table, preferred_element_type=jnp.float32)]
    broadcast_in_dim x4 -> x0, local copies, waits for them, and re-layouts: 3.92 us -> none  [the longest x3 3.85 us: sent_to_all(): copies = jnp.broadcast_to(value, (lax.axis_size(axis), *value.shape))]
    reduce_sum x5 -> x0, other arithmetic: 3.24 us -> none  [the longest x1 1.7 us: taken_together(): return sent_to_all(value, axis).sum(axis=0)]
    unnamed x18 -> x2, local copies, waits for them, and re-layouts: 0.06 us -> 2.5 us
    reshape x3 -> x0, local copies, waits for them, and re-layouts: 1.52 us -> none  [the longest x1 0.89 us: local(): jnp.concatenate([delta_q, delta_v], 1)]
  transfers between devices with their start and end apart: 4 -> 0, of which waited for: 4 -> 0; matrix products, arithmetic and copies ran while one was open for 3% -> 0% of each run, Pallas kernels for 0% -> 0%
where the time goes in v1:
time: 69.8 us; the launch traced here: 68.4 us
  Pallas kernels  65.3 us (94%)
  local copies, waits for them, and re-layouts  2.5 us (4%)
    pallas_call x1, Pallas kernels, local(): pl.pallas_call(functools.partial(kernel, dims), out_shape=(jax.ShapeDtype...  65.3 us
    unnamed x2, local copies, waits for them, and re-layouts  2.5 us

profile of v1, /device:TPU:1, one launch (start us, length us, event | category | flops | bytes accessed | tf_op | source)
XLA Modules:
  0.0 68.4 jit_solution(10768613099604343949)
XLA Ops:
  0.6 65.3 %shard_map.149 = (bf16[4,2,256]{2,1,0:T(2,128)(2,1)}, bf16[4,2,128]{2,1,0:T(2,128)(2,1)}) custom-call(bf16[4,2,4096]{2,1,0:T(2,128)(2,1)} %hidden.1, bf16[4,2,128]{2,1,0:T(2,128)(2,1)} %new_keys.1, bf16[4,1,512,128]{3,2,1,0:T(8,128)(2,1)} %key_cache.1, bf16[4,1,512,128]{3,2,1,0:T(8,128)(2,1)} %value_cache.1, s32[4]{0:T(128)} %cache_len.1, s32[4]{0:T(128)} %adapter_id.1, ...), custom_call_target="tpu_custom_call" | custom-call | tf_op jit(solution)/shard_map/pallas_call | solution.py:497
  65.9 1.3 %copy.18 = bf16[4,2,256]{2,1,0:T(2,128)(2,1)} copy(bf16[4,2,256]{2,1,0:T(2,128)(2,1)} %get-tuple-element.4) | data formatting | bytes 8192
  67.2 1.2 %copy.19 = bf16[4,2,128]{2,1,0:T(2,128)(2,1)} copy(bf16[4,2,128]{2,1,0:T(2,128)(2,1)} %get-tuple-element.5) | data formatting | bytes 4096

commit v2 on v1

v2 whole, which is shorter than its diff:
```python
import functools
import math

import jax
import jax.numpy as jnp
from jax import lax
from jax.experimental import pallas as pl
from jax.experimental.pallas import tpu as pltpu
from jax.sharding import PartitionSpec as P

MESH = pl.DeviceIdType.MESH
LANES = 128


def factors(wide):
    return (4, 4, wide // 16) if wide >= 32 else (2, 2, wide // 4)


def order_of(n):
    near = [d for d in (1, n - 1) if d < n]
    return list(dict.fromkeys(near + list(range(1, n))))


def kernel(
    dims,
    hidden,
    new_keys,
    key_cache,
    value_cache,
    cache_len,
    adapter_id,
    adapter_slot,
    adapter_rank,
    q_weight,
    v_weight,
    q_down,
    v_down,
    q_up,
    v_up,
    attended,
    new_values,
    hid,
    hid_part,
    h32,
    h16,
    kv,
    vv,
    nk,
    len_s,
    id_s,
    slot_s,
    rank_s,
    wq,
    wv,
    down,
    upq,
    upv,
    feats,
    mixed,
    arrive_p,
    red,
    delta,
    back,
    far_out,
    far_in,
    base,
    cos_t,
    sin_t,
    kn,
    vn,
    local_sem,
    f_send,
    f_recv,
    n_send,
    n_recv,
    rs_send,
    rs_recv,
    ag_send,
    ag_recv,
    b_send,
    b_recv,
    r_send,
    r_recv,
):
    ny, nn, nf, nt = dims
    near = ny * nn
    rows, _, width = hidden.shape
    toks = rows * 2
    part = width // nt
    slots = q_up.shape[0]
    rank_w = q_up.shape[1]
    q_w = q_up.shape[2]
    v_w = v_up.shape[2]
    cache = key_cache.shape[2]
    adapters = adapter_slot.shape[0]
    chunk = near * toks
    piece = chunk // nt
    bf, f32 = jnp.bfloat16, jnp.float32

    wide = lax.axis_index("wide")
    tp = lax.axis_index("tp")
    y = lax.div(wide, nf * nn)
    z = lax.rem(wide, nf * nn)
    zf = lax.div(z, nn)
    zn = lax.rem(z, nn)

    def turn(i, d, n):
        return lax.rem(i + d, n)

    def f_peer(d):
        return (y * (nf * nn) + turn(zf, d, nf) * nn + zn, tp)

    def n_peer(e):
        return (turn(y, e // nn, ny) * (nf * nn) + zf * nn + turn(zn, e % nn, nn), tp)

    def t_peer(e):
        return (wide, turn(tp, e, nt))

    def n_back(e):
        return (-(e // nn) % ny) * nn + (-(e % nn)) % nn

    loads = {}

    def load(name, src, dst, i):
        c = pltpu.make_async_copy(src, dst, local_sem.at[i])
        c.start()
        loads[name] = c

    def loaded(name):
        loads.pop(name).wait()

    col = pl.multiple_of(tp * part, part)
    load("hp", hidden.at[:, :, pl.ds(col, part)], hid_part, 0)
    load("id", adapter_id, id_s, 1)
    load("slot", adapter_slot, slot_s, 2)
    load("rank", adapter_rank, rank_s, 3)

    barrier = pltpu.get_barrier_semaphore()
    peers = (
        [f_peer(d) for d in order_of(nf)[::-1]]
        + [n_peer(e) for e in range(1, near)]
        + [t_peer(e) for e in range(1, nt)]
    )
    for p in peers:
        pl.semaphore_signal(barrier, inc=1, device_id=p, device_id_type=MESH)

    for name in ("id", "slot", "rank"):
        loaded(name)
    tok = lax.broadcasted_iota(jnp.int32, (toks, LANES), 0)
    lane = lax.broadcasted_iota(jnp.int32, (toks, LANES), 1)
    code = jnp.zeros((toks, LANES), jnp.int32)
    for r in range(rows):
        ident = id_s[r]
        mine = jnp.where(lax.rem(lane, rank_w) < rank_s[ident], slot_s[ident], adapters)
        code = jnp.where(lax.div(tok, 2) == r, mine, code)
    feats[0, 0, :, part:] = code.astype(f32).astype(bf)
    loaded("hp")
    for r in range(rows):
        h32[2 * r : 2 * r + 2, :part] = hid_part[r].astype(f32)
    feats[0, 0, :, :part] = h32[:, :part].astype(bf)

    def send(src, dst, ssem, rsem, peer):
        pltpu.make_async_remote_copy(
            src_ref=src,
            dst_ref=dst,
            send_sem=ssem,
            recv_sem=rsem,
            device_id=peer,
            device_id_type=MESH,
        ).start()

    def passed(ref, sem):
        pltpu.make_async_copy(ref, ref, sem).wait()

    pl.semaphore_wait(barrier, len(peers))

    for d in order_of(nf)[::-1]:
        send(feats.at[0, 0], feats.at[nf - d, 0], f_send.at[d], f_recv.at[nf - d], f_peer(d))

    def spread_near(d):
        if d:
            passed(feats.at[d, 0], f_recv.at[d])
        for e in range(1, near):
            send(feats.at[d, 0], feats.at[d, n_back(e)], n_send.at[d], n_recv.at[d], n_peer(e))

    def products(d):
        passed(feats.at[d, pl.ds(1, near - 1)], n_recv.at[d])
        x = feats[d, :, :, :part].reshape(chunk, part)
        place = feats[d, :, :, part:].reshape(chunk, LANES).astype(f32)
        place = place - (wide * slots).astype(f32)
        prod = lax.dot_general(x, down[...], (((1,), (1,)), ((), ())), preferred_element_type=f32)
        total = jnp.zeros((chunk, LANES), f32)
        for k in range(slots):
            total = jnp.where(place == float(k), prod[:, k * LANES : (k + 1) * LANES], total)
        mixed[d] = total.reshape(nt, piece, LANES)
        for e in range(1, nt):
            send(
                mixed.at[d, turn(tp, e, nt)],
                arrive_p.at[d, nt - e],
                rs_send.at[d],
                rs_recv.at[d],
                t_peer(e),
            )

    def reduce(d):
        passed(arrive_p.at[d, pl.ds(1, nt - 1)], rs_recv.at[d])
        total = mixed[d, tp]
        for e in range(1, nt):
            total = total + arrive_p[d, e]
        red[d, 0] = total.astype(bf)
        for e in range(1, nt):
            send(red.at[d, 0], red.at[d, nt - e], ag_send.at[d], ag_recv.at[d], t_peer(e))

    def expand(d):
        passed(red.at[d, pl.ds(1, nt - 1)], ag_recv.at[d])
        shrunk = jnp.concatenate(
            [red[d, turn(nt - tp, p, nt)].astype(f32) for p in range(nt)], 0
        )
        place = feats[d, :, :, part:].reshape(chunk, LANES).astype(f32)
        place = place - (wide * slots).astype(f32)
        spread = jnp.concatenate(
            [jnp.where(place == float(k), shrunk, 0.0).astype(bf) for k in range(slots)], 1
        )
        dq = jnp.dot(spread, upq[...], preferred_element_type=f32).astype(bf)
        dv = jnp.dot(spread, upv[...], preferred_element_type=f32).astype(bf)
        delta[d, :, :, :q_w] = dq.reshape(near, toks, q_w)
        delta[d, :, :, q_w:] = dv.reshape(near, toks, v_w)
        for e in range(1, near):
            send(delta.at[d, e], back.at[d, n_back(e)], b_send.at[d], b_recv.at[d], n_peer(e))

    def gather_back(d):
        passed(back.at[d, pl.ds(1, near - 1)], b_recv.at[d])
        total = delta[d, 0].astype(f32) + jnp.sum(back[d, 1:].astype(f32), 0)
        far_out[d] = total.astype(bf)
        if d:
            send(far_out.at[d], far_in.at[nf - d], r_send.at[d], r_recv.at[nf - d], f_peer(d))

    spread_near(0)

    load("hid", hidden, hid, 0)
    load("len", cache_len, len_s, 4)
    load("nk", new_keys, nk, 5)
    for k in range(slots):
        row = k * 2 * rank_w
        load(f"qd{k}", q_down.at[k], down.at[pl.ds(row, rank_w)], 8 + 4 * k)
        load(f"vd{k}", v_down.at[k], down.at[pl.ds(row + rank_w, rank_w)], 9 + 4 * k)
    load("wq", q_weight, wq, 6)
    load("wv", v_weight, wv, 7)
    upq[...] = jnp.zeros_like(upq)
    upv[...] = jnp.zeros_like(upv)
    for k in range(slots):
        row = k * 2 * rank_w
        load(f"qu{k}", q_up.at[k], upq.at[pl.ds(row, rank_w)], 10 + 4 * k)
        load(f"vu{k}", v_up.at[k], upv.at[pl.ds(row + rank_w, rank_w)], 11 + 4 * k)
    n0 = 8 + 4 * slots
    load("kc", key_cache, kv, n0)
    load("vc", value_cache, vv, n0 + 1)
    loaded("hid")
    for r in range(rows):
        h32[2 * r : 2 * r + 2, :] = hid[r].astype(f32)
    h16[...] = h32[...].astype(bf)
    loaded("len")
    position = lax.rem(tok, 2)
    for r in range(rows):
        position = position + jnp.where(lax.div(tok, 2) == r, len_s[r], 0)
    half = lax.rem(lane, 64)
    frequency = jnp.exp(-math.log(500000.0) * (2.0 * half.astype(f32) / 128))
    angle = position.astype(f32) * frequency
    cos_t[...] = jnp.cos(angle)
    sine = jnp.sin(angle)
    sin_t[...] = jnp.where(lane < 64, -sine, sine)
    kn[...] = jnp.zeros_like(kn)
    vn[...] = jnp.zeros_like(vn)
    loaded("nk")
    for r in range(rows):
        kn[2 * r : 2 * r + 2, :] = nk[r].astype(f32)

    order = order_of(nf)
    for d in order[:-1]:
        spread_near(d)
    for k in range(slots):
        loaded(f"qd{k}")
        loaded(f"vd{k}")
    products(0)
    spread_near(order[-1])
    for name in ("wq", "wv"):
        loaded(name)
    base[:, :q_w] = jnp.dot(h16[...], wq[...], preferred_element_type=f32)
    reduce(0)
    for d in order:
        products(d)
    for k in range(slots):
        loaded(f"qu{k}")
        loaded(f"vu{k}")
    expand(0)
    for d in order:
        reduce(d)
    base[:, q_w:] = jnp.dot(h16[...], wv[...], preferred_element_type=f32)
    gather_back(0)
    for d in order:
        expand(d)
    loaded("kc")
    loaded("vc")
    for d in order:
        gather_back(d)
    for d in range(nf):
        if d:
            passed(feats.at[0, 0], f_send.at[d])
        passed(feats.at[d, pl.ds(1, near - 1)], n_send.at[d])
        passed(arrive_p.at[d, pl.ds(1, nt - 1)], rs_send.at[d])
        passed(red.at[d, pl.ds(1, nt - 1)], ag_send.at[d])
        passed(back.at[d, pl.ds(1, near - 1)], b_send.at[d])
    total = far_out[0].astype(f32)
    for d in order:
        passed(far_in.at[d], r_recv.at[d])
        total = total + far_in[d].astype(f32)

    full = base[...] + total
    fresh = full[:, q_w:].astype(bf).astype(f32)
    vn[:toks, :] = fresh
    for r in range(rows):
        new_values[r] = fresh[2 * r : 2 * r + 2].astype(bf)
    heads = q_w // LANES
    turned = []
    for h in range(heads):
        x = full[:, h * LANES : (h + 1) * LANES]
        turned.append(x * cos_t[...] + pltpu.roll(x, 64, 1) * sin_t[...])
    queries = jnp.concatenate(turned, 0).astype(bf)
    many = heads * toks
    inv_root = 1.0 / math.sqrt(LANES)
    row_id = lax.broadcasted_iota(jnp.int32, (many, cache), 0)
    row_of = lax.div(lax.rem(row_id, toks), 2)
    spot = lax.broadcasted_iota(jnp.int32, (many, cache), 1)
    contract = (((1,), (1,)), ((), ()))
    scores = jnp.zeros((many, cache), f32)
    length = jnp.zeros((many, cache), jnp.int32)
    for r in range(rows):
        one = lax.dot_general(queries, kv[r, 0], contract, preferred_element_type=f32)
        scores = jnp.where(row_of == r, one, scores)
        length = jnp.where(row_of == r, len_s[r], length)
    scores = jnp.where(spot < length, scores * inv_root, -jnp.inf)
    fresh_scores = (
        lax.dot_general(queries, kn[...].astype(bf), contract, preferred_element_type=f32)
        * inv_root
    )
    row_n = lax.rem(lax.broadcasted_iota(jnp.int32, fresh_scores.shape, 0), toks)
    col_n = lax.broadcasted_iota(jnp.int32, fresh_scores.shape, 1)
    seen = (lax.div(row_n, 2) == lax.div(col_n, 2)) & (lax.rem(col_n, 2) <= lax.rem(row_n, 2))
    fresh_scores = jnp.where(seen, fresh_scores, -jnp.inf)
    largest = jnp.maximum(
        jnp.max(scores, -1, keepdims=True), jnp.max(fresh_scores, -1, keepdims=True)
    )
    old_weight = jnp.exp(scores - largest)
    new_weight = jnp.exp(fresh_scores - largest)
    denominator = jnp.sum(old_weight, -1, keepdims=True) + jnp.sum(new_weight, -1, keepdims=True)
    old_prob = old_weight / denominator
    new_prob = (new_weight / denominator).astype(bf)
    result = jnp.dot(new_prob, vn[...].astype(bf), preferred_element_type=f32)
    for r in range(rows):
        weights = jnp.where(row_of == r, old_prob, 0.0).astype(bf)
        result = result + jnp.dot(weights, vv[r, 0], preferred_element_type=f32)
    for r in range(rows):
        for h in range(heads):
            at = h * toks + 2 * r
            attended[r, :, h * LANES : (h + 1) * LANES] = result[at : at + 2].astype(bf)
    for d in order:
        passed(far_out.at[d], r_send.at[d])


def local(dims, *args):
    (hidden, new_keys, key_cache, value_cache, cache_len, adapter_id, adapter_slot, adapter_rank,
     q_weight, v_weight, q_down, v_down, q_up, v_up) = args
    ny, nn, nf, nt = dims
    near = ny * nn
    rows, _, width = hidden.shape
    toks = rows * 2
    part = width // nt
    slots, rank_w, q_w = q_up.shape
    v_w = v_up.shape[2]
    all_w = q_w + v_w
    piece = near * toks // nt
    bf, f32, i32 = jnp.bfloat16, jnp.float32, jnp.int32
    V = pltpu.VMEM
    dma = pltpu.SemaphoreType.DMA
    q_down = jnp.swapaxes(q_down, 1, 2)
    v_down = jnp.swapaxes(v_down, 1, 2)
    scratch = [
        V((rows, 2, width), bf),
        V((rows, 2, part), bf),
        V((toks, width), f32),
        V((toks, width), bf),
        V(key_cache.shape, bf),
        V(value_cache.shape, bf),
        V(new_keys.shape, bf),
        pltpu.SMEM(cache_len.shape, i32),
        pltpu.SMEM(adapter_id.shape, i32),
        pltpu.SMEM(adapter_slot.shape, i32),
        pltpu.SMEM(adapter_rank.shape, i32),
        V(q_weight.shape, bf),
        V(v_weight.shape, bf),
        V((slots * 2 * rank_w, part), bf),
        V((slots * 2 * rank_w, q_w), bf),
        V((slots * 2 * rank_w, v_w), bf),
        V((nf, near, toks, part + LANES), bf),
        V((nf, nt, piece, LANES), f32),
        V((nf, nt, piece, LANES), f32),
        V((nf, nt, piece, LANES), bf),
        V((nf, near, toks, all_w), bf),
        V((nf, near, toks, all_w), bf),
        V((nf, toks, all_w), bf),
        V((nf, toks, all_w), bf),
        V((toks, all_w), f32),
        V((toks, LANES), f32),
        V((toks, LANES), f32),
        V((LANES, LANES), f32),
        V((LANES, LANES), f32),
        dma((8 + 4 * slots + 2,)),
    ]
    scratch += [dma((nf,)) for _ in range(12)]
    any_space = pl.BlockSpec(memory_space=pl.ANY)
    vmem = pl.BlockSpec(memory_space=pltpu.VMEM)
    return tuple(
        pl.pallas_call(
            functools.partial(kernel, dims),
            out_shape=(
                jax.ShapeDtypeStruct((rows, 2, q_w), bf),
                jax.ShapeDtypeStruct((rows, 2, v_w), bf),
            ),
            in_specs=[any_space] * 14,
            out_specs=(vmem, vmem),
            scratch_shapes=scratch,
            compiler_params=pltpu.CompilerParams(
                collective_id=0, has_side_effects=True, vmem_limit_bytes=56 * 1024 * 1024
            ),
        )(hidden, new_keys, key_cache, value_cache, cache_len, adapter_id, adapter_slot,
          adapter_rank, q_weight, v_weight, q_down, v_down, q_up, v_up)
    )


def solution(mesh):
    dims = factors(mesh.shape["wide"]) + (mesh.shape["tp"],)
    return jax.shard_map(
        functools.partial(local, dims),
        mesh=mesh,
        in_specs=(
            P("wide", None, None),
            P("wide", None, "tp"),
            P("wide", "tp", None, None),
            P("wide", "tp", None, None),
            P("wide"),
            P("wide"),
            P(),
            P(),
            P(None, "tp"),
            P(None, "tp"),
            P("wide", "tp", None),
            P("wide", "tp", None),
            P("wide", None, "tp"),
            P("wide", None, "tp"),
        ),
        out_specs=(P("wide", None, "tp"), P("wide", None, "tp")),
        check_vma=False,
    )
```

time: 69.8 us -> 59 us (0.85)
  Pallas kernels: 65.3 us -> 54.7 us
    pallas_call x1, Pallas kernels: 65.3 us -> 54.7 us  [local(): pl.pallas_call(functools.partial(kernel, dims), out_shape=(jax.ShapeDtype...]
where the time goes in v2:
time: 59 us; the launch traced here: 57.9 us
  Pallas kernels  54.7 us (93%)
  local copies, waits for them, and re-layouts  2.5 us (4%)
  between operations  0.64 us (1%)
    pallas_call x1, Pallas kernels, local(): pl.pallas_call(functools.partial(kernel, dims), out_shape=(jax.ShapeDtype...  54.7 us
    unnamed x2, local copies, waits for them, and re-layouts  2.5 us

profile of v2, /device:TPU:1, one launch (start us, length us, event | category | flops | bytes accessed | tf_op | source)
XLA Modules:
  0.0 57.9 jit_solution(11088913338523192197)
XLA Ops:
  0.6 54.7 %shard_map.149 = (bf16[4,2,256]{2,1,0:T(2,128)(2,1)}, bf16[4,2,128]{2,1,0:T(2,128)(2,1)}) custom-call(bf16[4,2,4096]{2,1,0:T(2,128)(2,1)} %hidden.1, bf16[4,2,128]{2,1,0:T(2,128)(2,1)} %new_keys.1, bf16[4,1,512,128]{3,2,1,0:T(8,128)(2,1)} %key_cache.1, bf16[4,1,512,128]{3,2,1,0:T(8,128)(2,1)} %value_cache.1, s32[4]{0:T(128)} %cache_len.1, s32[4]{0:T(128)} %adapter_id.1, ...), custom_call_target="tpu_custom_call" | custom-call | tf_op jit(solution)/shard_map/pallas_call | solution.py:423
  55.4 1.3 %copy.18 = bf16[4,2,256]{2,1,0:T(2,128)(2,1)} copy(bf16[4,2,256]{2,1,0:T(2,128)(2,1)} %get-tuple-element.4) | data formatting | bytes 8192
  56.6 1.2 %copy.19 = bf16[4,2,128]{2,1,0:T(2,128)(2,1)} copy(bf16[4,2,128]{2,1,0:T(2,128)(2,1)} %get-tuple-element.5) | data formatting | bytes 4096

commit v3 on v2

--- a/solution.py
+++ b/solution.py
@@ -99,19 +99,25 @@
 
     wide = lax.axis_index("wide")
     tp = lax.axis_index("tp")
-    y = lax.div(wide, nf * nn)
-    z = lax.rem(wide, nf * nn)
-    zf = lax.div(z, nn)
-    zn = lax.rem(z, nn)
+    nz = nf * nn
+    y = lax.div(wide, nz)
+    z = lax.rem(wide, nz)
 
     def turn(i, d, n):
         return lax.rem(i + d, n)
 
     def f_peer(d):
-        return (y * (nf * nn) + turn(zf, d, nf) * nn + zn, tp)
+        return (y * nz + turn(z, d * nn, nz), tp)
+
+    even = lax.rem(z, 2) == 0
+    steps = (0, 1, jnp.where(even, 2, nz - 2), nz - 1) if nn == 4 else (0, jnp.where(even, 1, nz - 1))
+    homes = tuple(nz - s if i == 2 else s for i, s in enumerate(steps))
 
     def n_peer(e):
-        return (turn(y, e // nn, ny) * (nf * nn) + zf * nn + turn(zn, e % nn, nn), tp)
+        return (turn(y, e // nn, ny) * nz + turn(z, steps[e % nn], nz), tp)
+
+    def h_peer(e):
+        return (turn(y, e // nn, ny) * nz + turn(z, homes[e % nn], nz), tp)
 
     def t_peer(e):
         return (wide, turn(tp, e, nt))
@@ -139,6 +145,7 @@
     peers = (
         [f_peer(d) for d in order_of(nf)[::-1]]
         + [n_peer(e) for e in range(1, near)]
+        + [h_peer(e) for e in range(1, near) if e % nn == 2]
         + [t_peer(e) for e in range(1, nt)]
     )
     for p in peers:
@@ -226,7 +233,7 @@
         delta[d, :, :, :q_w] = dq.reshape(near, toks, q_w)
         delta[d, :, :, q_w:] = dv.reshape(near, toks, v_w)
         for e in range(1, near):
-            send(delta.at[d, e], back.at[d, n_back(e)], b_send.at[d], b_recv.at[d], n_peer(e))
+            send(delta.at[d, e], back.at[d, n_back(e)], b_send.at[d], b_recv.at[d], h_peer(e))
 
     def gather_back(d):
         passed(back.at[d, pl.ds(1, near - 1)], b_recv.at[d])

time: 59 us -> 54.4 us (0.922)
  Pallas kernels: 54.7 us -> 50.4 us
    pallas_call x1, Pallas kernels: 54.7 us -> 50.4 us  [local(): pl.pallas_call(functools.partial(kernel, dims), out_shape=(jax.ShapeDtype...]
where the time goes in v3:
time: 54.4 us; the launch traced here: 53.5 us
  Pallas kernels  50.4 us (93%)
  local copies, waits for them, and re-layouts  2.5 us (5%)
  between operations  0.64 us (1%)
    pallas_call x1, Pallas kernels, local(): pl.pallas_call(functools.partial(kernel, dims), out_shape=(jax.ShapeDtype...  50.4 us
    unnamed x2, local copies, waits for them, and re-layouts  2.5 us

profile of v3, /device:TPU:1, one launch (start us, length us, event | category | flops | bytes accessed | tf_op | source)
XLA Modules:
  0.0 53.5 jit_solution(10916257383445314291)
XLA Ops:
  0.6 50.4 %shard_map.149 = (bf16[4,2,256]{2,1,0:T(2,128)(2,1)}, bf16[4,2,128]{2,1,0:T(2,128)(2,1)}) custom-call(bf16[4,2,4096]{2,1,0:T(2,128)(2,1)} %hidden.1, bf16[4,2,128]{2,1,0:T(2,128)(2,1)} %new_keys.1, bf16[4,1,512,128]{3,2,1,0:T(8,128)(2,1)} %key_cache.1, bf16[4,1,512,128]{3,2,1,0:T(8,128)(2,1)} %value_cache.1, s32[4]{0:T(128)} %cache_len.1, s32[4]{0:T(128)} %adapter_id.1, ...), custom_call_target="tpu_custom_call" | custom-call | tf_op jit(solution)/shard_map/pallas_call | solution.py:430
  51.0 1.3 %copy.18 = bf16[4,2,256]{2,1,0:T(2,128)(2,1)} copy(bf16[4,2,256]{2,1,0:T(2,128)(2,1)} %get-tuple-element.4) | data formatting | bytes 8192
  52.3 1.2 %copy.19 = bf16[4,2,128]{2,1,0:T(2,128)(2,1)} copy(bf16[4,2,128]{2,1,0:T(2,128)(2,1)} %get-tuple-element.5) | data formatting | bytes 4096

commit v4 on v3

--- a/solution.py
+++ b/solution.py
@@ -13,12 +13,7 @@
 
 
 def factors(wide):
-    return (4, 4, wide // 16) if wide >= 32 else (2, 2, wide // 4)
-
-
-def order_of(n):
-    near = [d for d in (1, n - 1) if d < n]
-    return list(dict.fromkeys(near + list(range(1, n))))
+    return (4, 4, wide // 16) if wide >= 32 else (1, 4, wide // 4)
 
 
 def kernel(
@@ -55,6 +50,7 @@
     down,
     upq,
     upv,
+    own,
     feats,
     mixed,
     arrive_p,
@@ -107,7 +103,7 @@
         return lax.rem(i + d, n)
 
     def f_peer(d):
-        return (y * nz + turn(z, d * nn, nz), tp)
+        return (y * nz + turn(z, d * nn + 2, nz), tp)
 
     even = lax.rem(z, 2) == 0
     steps = (0, 1, jnp.where(even, 2, nz - 2), nz - 1) if nn == 4 else (0, jnp.where(even, 1, nz - 1))
@@ -124,6 +120,12 @@
 
     def n_back(e):
         return (-(e // nn) % ny) * nn + (-(e % nn)) % nn
+
+    order = sorted(range(nf), key=lambda d: min(d * nn + 2, nz - d * nn - 2))
+    near_order = sorted(
+        range(1, near), key=lambda e: -min(e // nn, ny - e // nn) - min(e % nn, nn - e % nn)
+    )
+    tp_order = sorted(range(1, nt), key=lambda e: -min(e, nt - e))
 
     loads = {}
 
@@ -143,10 +145,10 @@
 
     barrier = pltpu.get_barrier_semaphore()
     peers = (
-        [f_peer(d) for d in order_of(nf)[::-1]]
-        + [n_peer(e) for e in range(1, near)]
-        + [h_peer(e) for e in range(1, near) if e % nn == 2]
-        + [t_peer(e) for e in range(1, nt)]
+        [f_peer(d) for d in order[::-1]]
+        + [n_peer(e) for e in near_order]
+        + [h_peer(e) for e in near_order if e % nn == 2]
+        + [t_peer(e) for e in tp_order]
     )
     for p in peers:
         pl.semaphore_signal(barrier, inc=1, device_id=p, device_id_type=MESH)
@@ -160,11 +162,11 @@
         ident = id_s[r]
         mine = jnp.where(lax.rem(lane, rank_w) < rank_s[ident], slot_s[ident], adapters)
         code = jnp.where(lax.div(tok, 2) == r, mine, code)
-    feats[0, 0, :, part:] = code.astype(f32).astype(bf)
+    own[:, part:] = code.astype(f32).astype(bf)
     loaded("hp")
     for r in range(rows):
         h32[2 * r : 2 * r + 2, :part] = hid_part[r].astype(f32)
-    feats[0, 0, :, :part] = h32[:, :part].astype(bf)
+    own[:, :part] = h32[:, :part].astype(bf)
 
     def send(src, dst, ssem, rsem, peer):
         pltpu.make_async_remote_copy(
@@ -181,13 +183,13 @@
 
     pl.semaphore_wait(barrier, len(peers))
 
-    for d in order_of(nf)[::-1]:
-        send(feats.at[0, 0], feats.at[nf - d, 0], f_send.at[d], f_recv.at[nf - d], f_peer(d))
+    for d in order[::-1]:
+        there = nf - 1 - d
+        send(own, feats.at[there, 0], f_send.at[d], f_recv.at[there], f_peer(d))
 
     def spread_near(d):
-        if d:
-            passed(feats.at[d, 0], f_recv.at[d])
-        for e in range(1, near):
+        passed(feats.at[d, 0], f_recv.at[d])
+        for e in near_order:
             send(feats.at[d, 0], feats.at[d, n_back(e)], n_send.at[d], n_recv.at[d], n_peer(e))
 
     def products(d):
@@ -200,7 +202,7 @@
         for k in range(slots):
             total = jnp.where(place == float(k), prod[:, k * LANES : (k + 1) * LANES], total)
         mixed[d] = total.reshape(nt, piece, LANES)
-        for e in range(1, nt):
+        for e in tp_order:
             send(
                 mixed.at[d, turn(tp, e, nt)],
                 arrive_p.at[d, nt - e],
@@ -215,7 +217,7 @@
         for e in range(1, nt):
             total = total + arrive_p[d, e]
         red[d, 0] = total.astype(bf)
-        for e in range(1, nt):
+        for e in tp_order:
             send(red.at[d, 0], red.at[d, nt - e], ag_send.at[d], ag_recv.at[d], t_peer(e))
 
     def expand(d):
@@ -232,17 +234,15 @@
         dv = jnp.dot(spread, upv[...], preferred_element_type=f32).astype(bf)
         delta[d, :, :, :q_w] = dq.reshape(near, toks, q_w)
         delta[d, :, :, q_w:] = dv.reshape(near, toks, v_w)
-        for e in range(1, near):
+        for e in near_order:
             send(delta.at[d, e], back.at[d, n_back(e)], b_send.at[d], b_recv.at[d], h_peer(e))
 
     def gather_back(d):
         passed(back.at[d, pl.ds(1, near - 1)], b_recv.at[d])
         total = delta[d, 0].astype(f32) + jnp.sum(back[d, 1:].astype(f32), 0)
         far_out[d] = total.astype(bf)
-        if d:
-            send(far_out.at[d], far_in.at[nf - d], r_send.at[d], r_recv.at[nf - d], f_peer(d))
-
-    spread_near(0)
+        there = nf - 1 - d
+        send(far_out.at[d], far_in.at[there], r_send.at[d], r_recv.at[there], f_peer(d))
 
     load("hid", hidden, hid, 0)
     load("len", cache_len, len_s, 4)
@@ -282,28 +282,22 @@
     for r in range(rows):
         kn[2 * r : 2 * r + 2, :] = nk[r].astype(f32)
 
-    order = order_of(nf)
-    for d in order[:-1]:
+    for d in order:
         spread_near(d)
+    for name in ("wq", "wv"):
+        loaded(name)
+    base[:, :q_w] = jnp.dot(h16[...], wq[...], preferred_element_type=f32)
     for k in range(slots):
         loaded(f"qd{k}")
         loaded(f"vd{k}")
-    products(0)
-    spread_near(order[-1])
-    for name in ("wq", "wv"):
-        loaded(name)
-    base[:, :q_w] = jnp.dot(h16[...], wq[...], preferred_element_type=f32)
-    reduce(0)
     for d in order:
         products(d)
+    base[:, q_w:] = jnp.dot(h16[...], wv[...], preferred_element_type=f32)
     for k in range(slots):
         loaded(f"qu{k}")
         loaded(f"vu{k}")
-    expand(0)
     for d in order:
         reduce(d)
-    base[:, q_w:] = jnp.dot(h16[...], wv[...], preferred_element_type=f32)
-    gather_back(0)
     for d in order:
         expand(d)
     loaded("kc")
@@ -311,13 +305,12 @@
     for d in order:
         gather_back(d)
     for d in range(nf):
-        if d:
-            passed(feats.at[0, 0], f_send.at[d])
+        passed(own, f_send.at[d])
         passed(feats.at[d, pl.ds(1, near - 1)], n_send.at[d])
         passed(arrive_p.at[d, pl.ds(1, nt - 1)], rs_send.at[d])
         passed(red.at[d, pl.ds(1, nt - 1)], ag_send.at[d])
         passed(back.at[d, pl.ds(1, near - 1)], b_send.at[d])
-    total = far_out[0].astype(f32)
+    total = jnp.zeros((toks, q_w + v_w), f32)
     for d in order:
         passed(far_in.at[d], r_recv.at[d])
         total = total + far_in[d].astype(f32)
@@ -408,6 +401,7 @@
         V((slots * 2 * rank_w, part), bf),
         V((slots * 2 * rank_w, q_w), bf),
         V((slots * 2 * rank_w, v_w), bf),
+        V((toks, part + LANES), bf),
         V((nf, near, toks, part + LANES), bf),
         V((nf, nt, piece, LANES), f32),
         V((nf, nt, piece, LANES), f32),

time: 54.4 us -> 50.9 us (0.936); the launches traced: 53.5 us -> 50.7 us
  Pallas kernels: 50.4 us -> 47.5 us
    pallas_call x1, Pallas kernels: 50.4 us -> 47.5 us  [local(): pl.pallas_call(functools.partial(kernel, dims), out_shape=(jax.ShapeDtype...]
where the time goes in v4:
time: 50.9 us; the launch traced here: 50.7 us
  Pallas kernels  47.5 us (93%)
  local copies, waits for them, and re-layouts  2.5 us (5%)
  between operations  0.64 us (1%)
    pallas_call x1, Pallas kernels, local(): pl.pallas_call(functools.partial(kernel, dims), out_shape=(jax.ShapeDtype...  47.5 us
    unnamed x2, local copies, waits for them, and re-layouts  2.5 us

profile of v4, /device:TPU:1, one launch (start us, length us, event | category | flops | bytes accessed | tf_op | source)
XLA Modules:
  0.0 50.7 jit_solution(10176109739757685735)
XLA Ops:
  0.6 47.5 %shard_map.149 = (bf16[4,2,256]{2,1,0:T(2,128)(2,1)}, bf16[4,2,128]{2,1,0:T(2,128)(2,1)}) custom-call(bf16[4,2,4096]{2,1,0:T(2,128)(2,1)} %hidden.1, bf16[4,2,128]{2,1,0:T(2,128)(2,1)} %new_keys.1, bf16[4,1,512,128]{3,2,1,0:T(8,128)(2,1)} %key_cache.1, bf16[4,1,512,128]{3,2,1,0:T(8,128)(2,1)} %value_cache.1, s32[4]{0:T(128)} %cache_len.1, s32[4]{0:T(128)} %adapter_id.1, ...), custom_call_target="tpu_custom_call" | custom-call | tf_op jit(solution)/shard_map/pallas_call | solution.py:424
  48.2 1.3 %copy.18 = bf16[4,2,256]{2,1,0:T(2,128)(2,1)} copy(bf16[4,2,256]{2,1,0:T(2,128)(2,1)} %get-tuple-element.4) | data formatting | bytes 8192
  49.5 1.2 %copy.19 = bf16[4,2,128]{2,1,0:T(2,128)(2,1)} copy(bf16[4,2,128]{2,1,0:T(2,128)(2,1)} %get-tuple-element.5) | data formatting | bytes 4096

commit v5 on v4

--- a/solution.py
+++ b/solution.py
@@ -32,6 +32,8 @@
     v_down,
     q_up,
     v_up,
+    attended_out,
+    new_values_out,
     attended,
     new_values,
     hid,
@@ -320,6 +322,7 @@
     vn[:toks, :] = fresh
     for r in range(rows):
         new_values[r] = fresh[2 * r : 2 * r + 2].astype(bf)
+    load("nv", new_values, new_values_out, 0)
     heads = q_w // LANES
     turned = []
     for h in range(heads):
@@ -363,8 +366,22 @@
         for h in range(heads):
             at = h * toks + 2 * r
             attended[r, :, h * LANES : (h + 1) * LANES] = result[at : at + 2].astype(bf)
+    load("at", attended, attended_out, 1)
     for d in order:
         passed(far_out.at[d], r_send.at[d])
+    loaded("nv")
+    loaded("at")
+
+
+def write_out(a, b, out_a, out_b, sems):
+    copies = [
+        pltpu.make_async_copy(a, out_a, sems.at[0]),
+        pltpu.make_async_copy(b, out_b, sems.at[1]),
+    ]
+    for c in copies:
+        c.start()
+    for c in copies:
+        c.wait()
 
 
 def local(dims, *args):
@@ -385,6 +402,8 @@
     q_down = jnp.swapaxes(q_down, 1, 2)
     v_down = jnp.swapaxes(v_down, 1, 2)
     scratch = [
+        V((rows, 2, q_w), bf),
+        V((rows, 2, v_w), bf),
         V((rows, 2, width), bf),
         V((rows, 2, part), bf),
         V((toks, width), f32),
@@ -419,16 +438,16 @@
     ]
     scratch += [dma((nf,)) for _ in range(12)]
     any_space = pl.BlockSpec(memory_space=pl.ANY)
-    vmem = pl.BlockSpec(memory_space=pltpu.VMEM)
-    return tuple(
+    shapes = (
+        jax.ShapeDtypeStruct((rows, 2, q_w), bf),
+        jax.ShapeDtypeStruct((rows, 2, v_w), bf),
+    )
+    outs = (
         pl.pallas_call(
             functools.partial(kernel, dims),
-            out_shape=(
-                jax.ShapeDtypeStruct((rows, 2, q_w), bf),
-                jax.ShapeDtypeStruct((rows, 2, v_w), bf),
-            ),
+            out_shape=shapes,
             in_specs=[any_space] * 14,
-            out_specs=(vmem, vmem),
+            out_specs=(any_space, any_space),
             scratch_shapes=scratch,
             compiler_params=pltpu.CompilerParams(
                 collective_id=0, has_side_effects=True, vmem_limit_bytes=56 * 1024 * 1024
@@ -436,6 +455,14 @@
         )(hidden, new_keys, key_cache, value_cache, cache_len, adapter_id, adapter_slot,
           adapter_rank, q_weight, v_weight, q_down, v_down, q_up, v_up)
     )
+    return pl.pallas_call(
+        write_out,
+        out_shape=shapes,
+        in_specs=[any_space] * 2,
+        out_specs=(any_space, any_space),
+        scratch_shapes=[dma((2,))],
+        compiler_params=pltpu.CompilerParams(vmem_limit_bytes=56 * 1024 * 1024),
+    )(*outs)
 
 
 def solution(mesh):

time: 50.9 us -> 49.6 us (0.974)
  local copies, waits for them, and re-layouts: 2.5 us -> 0 us
  Pallas kernels: 47.5 us -> 48.8 us
    unnamed x2 -> x0, local copies, waits for them, and re-layouts: 2.5 us -> none
    pallas_call x1 -> x2, Pallas kernels: 47.5 us -> 48.8 us  [the longest x1 47.5 us: local(): pl.pallas_call(functools.partial(kernel, dims), out_shape=shapes, in_spec...]
where the time goes in v5:
time: 49.6 us; the launch traced here: 49.5 us
  Pallas kernels  48.8 us (98%)
  between operations  0.64 us (1%)
    pallas_call x1, Pallas kernels, local(): pl.pallas_call(functools.partial(kernel, dims), out_shape=shapes, in_spec...  47.5 us
    pallas_call x1, Pallas kernels, local(): pl.pallas_call(write_out, out_shape=shapes, in_specs=[any_space] * 2, out...  1.31 us

profile of v5, /device:TPU:1, one launch (start us, length us, event | category | flops | bytes accessed | tf_op | source)
XLA Modules:
  0.0 49.5 jit_solution(15714963894281532150)
XLA Ops:
  0.6 47.5 %shard_map.149 = (bf16[4,2,256]{2,1,0:T(2,128)(2,1)}, bf16[4,2,128]{2,1,0:T(2,128)(2,1)}) custom-call(bf16[4,2,4096]{2,1,0:T(2,128)(2,1)} %hidden.1, bf16[4,2,128]{2,1,0:T(2,128)(2,1)} %new_keys.1, bf16[4,1,512,128]{3,2,1,0:T(8,128)(2,1)} %key_cache.1, bf16[4,1,512,128]{3,2,1,0:T(8,128)(2,1)} %value_cache.1, s32[4]{0:T(128)} %cache_len.1, s32[4]{0:T(128)} %adapter_id.1, ...), custom_call_target="tpu_custom_call" | custom-call | tf_op jit(solution)/shard_map/pallas_call | solution.py:446
  48.2 1.3 %shard_map.150 = (bf16[4,2,256]{2,1,0:T(2,128)(2,1)}, bf16[4,2,128]{2,1,0:T(2,128)(2,1)}) custom-call(bf16[4,2,256]{2,1,0:T(2,128)(2,1)} %get-tuple-element.4.a, bf16[4,2,128]{2,1,0:T(2,128)(2,1)} %get-tuple-element.5.b), custom_call_target="tpu_custom_call" | custom-call | tf_op jit(solution)/shard_map/pallas_call | solution.py:458
